TPU v7x, 32 devices: a whole 2x2x4 slice. The times are simulated.
32 devices in a mesh: dp: 2 (over y), expert: 16 (over z, x, core).
Axes of the slice: x: 2, y: 2, z: 4, core: 2. Of those that a mesh axis runs over, the one named last changes fastest.
Arguments:
- activations: bfloat16 [4096, 4096], P(('dp', 'expert')), may hold values from -6 to 6
- cotangent: bfloat16 [4096, 4096], P(('dp', 'expert')), may hold values from -6 to 6
- expert_ids: int32 [4096, 1], P(('dp', 'expert')), may hold values from 0 to 127; in each aligned block of 128 rows (0 to 127, 128 to 255, ...) at most 2 rows name the same one
- gate_probs: float32 [4096, 1], P(('dp', 'expert')), may hold values from 0.2 to 1
- gate_up: bfloat16 [16, 2, 4096, 1536], P('expert', None, None, 'dp'), may hold values from -0.09375 to 0.09375
- down_proj: bfloat16 [16, 1536, 4096], P('expert', 'dp'), may hold values from -0.15625 to 0.15625
Outputs:
- input_grad: bfloat16 [4096, 4096], P(('dp', 'expert'))
- grad_gate_up: bfloat16 [16, 2, 4096, 1536], P('expert', None, None, 'dp')
- grad_down: bfloat16 [16, 1536, 4096], P('expert', 'dp')
Inputs may be any that keep to these rules, and one draw needn't show every extreme that they name: `expert_ids`: expert e < 16 is held by index e of the expert axis. Among the 128 tokens of one device no expert is named more than 2 times, a bound that some block reaches.
All inputs are finite; a program needn't handle non-finite values.
Results may differ from a plain program's by a relative error of at most 0.0058.
Values may be sent and summed in bfloat16 or wider, within the bound.
No kernel may reach another device: no remote copies, remote signals or barrier semaphores. Data moves between devices by JAX's collectives and lax.ppermute only.
A program may use at most 128 MiB of HBM per device.

v0:
```python
import functools

import jax
import jax.numpy as jnp
from jax import lax
from jax.experimental import pallas as pl
from jax.experimental.pallas import tpu as pltpu
from jax.sharding import PartitionSpec as P

CAP = 2
MIB = 1024 * 1024
VMEM = pl.BlockSpec(memory_space=pltpu.VMEM)
HBM = pl.BlockSpec(memory_space=pltpu.HBM)


def dot_nn(a, b):
    return lax.dot_general(a, b, (((1,), (0,)), ((), ())), preferred_element_type=jnp.float32)


def dot_nt(a, b):
    return lax.dot_general(a, b, (((1,), (1,)), ((), ())), preferred_element_type=jnp.float32)


def dot_tn(a, b):
    return lax.dot_general(a, b, (((0,), (0,)), ((), ())), preferred_element_type=jnp.float32)


def cost(flops, moved):
    return pl.CostEstimate(flops=int(flops), bytes_accessed=int(moved), transcendentals=0)


def params(mib):
    return pltpu.CompilerParams(vmem_limit_bytes=mib * MIB)


def in_hbm(value):
    return pltpu.with_memory_space_constraint(value, pltpu.HBM)


def bf16(*shape):
    return jax.ShapeDtypeStruct(shape, jnp.bfloat16)


def route_kernel(experts, chunk, ids_hbm, probs_hbm, act_hbm, cot_hbm, *refs):
    send_tok, send_cot, place_ref, ids_ref, probs_ref, act, cot, sems = refs
    tokens, width = act.shape
    steps = width // chunk
    small = (
        pltpu.make_async_copy(ids_hbm, ids_ref, sems.at[2 * steps]),
        pltpu.make_async_copy(probs_hbm, probs_ref, sems.at[2 * steps + 1]),
    )
    large = []
    for step in range(steps):
        at = pl.ds(step * chunk, chunk)
        large.append(
            (
                pltpu.make_async_copy(act_hbm.at[:, at], act.at[:, at], sems.at[2 * step]),
                pltpu.make_async_copy(cot_hbm.at[:, at], cot.at[:, at], sems.at[2 * step + 1]),
            )
        )
    for one in small:
        one.start()
    for pair in large:
        for one in pair:
            one.start()
    for one in small:
        one.wait()

    ids = ids_ref[...]
    inside = ids < experts
    near = jnp.where(inside, ids, -CAP)
    units = lax.broadcasted_iota(jnp.int32, (experts, tokens), 0)
    onehot = jnp.where(units == near, 1.0, 0.0)
    earlier = lax.broadcasted_iota(jnp.int32, (tokens, tokens), 0) < lax.broadcasted_iota(
        jnp.int32, (tokens, tokens), 1
    )
    before = dot_nn(onehot.astype(jnp.bfloat16), jnp.where(earlier, 1.0, 0.0).astype(jnp.bfloat16))
    rank = jnp.sum(before * onehot, axis=0, keepdims=True).astype(jnp.int32)
    slots = lax.broadcasted_iota(jnp.int32, (experts * CAP, tokens), 0)
    place = jnp.where(slots == near * CAP + rank, 1.0, 0.0)
    weight = jnp.sum(place * probs_ref[...], axis=1, keepdims=True)
    place = place.astype(jnp.bfloat16)
    place_ref[...] = place
    for step in range(steps):
        at = slice(step * chunk, (step + 1) * chunk)
        for one in large[step]:
            one.wait()
        rows_tok = dot_nn(place, act[:, at]).astype(jnp.bfloat16)
        rows_cot = (weight * dot_nn(place, cot[:, at])).astype(jnp.bfloat16)
        for unit in range(experts):
            send_tok[unit, :, at] = rows_tok[unit * CAP : (unit + 1) * CAP]
            send_cot[unit, :, at] = rows_cot[unit * CAP : (unit + 1) * CAP]


def route(ids, probs, act, cot, experts):
    tokens, width = act.shape
    chunk = min(1024, width)
    return pl.pallas_call(
        functools.partial(route_kernel, experts, chunk),
        in_specs=[HBM] * 4,
        out_specs=[VMEM] * 3,
        out_shape=[bf16(experts, CAP, width)] * 2 + [bf16(experts * CAP, tokens)],
        scratch_shapes=[
            pltpu.VMEM((1, tokens), jnp.int32),
            pltpu.VMEM((1, tokens), jnp.float32),
            pltpu.VMEM((tokens, width), jnp.bfloat16),
            pltpu.VMEM((tokens, width), jnp.bfloat16),
            pltpu.SemaphoreType.DMA((2 * (width // chunk) + 2,)),
        ],
        compiler_params=params(16),
        cost_estimate=cost(4 * experts * CAP * tokens * width, 4 * tokens * width),
        name="route_rows",
    )(in_hbm(ids), in_hbm(probs), in_hbm(act), in_hbm(cot))


def forward_kernel(groups, chunk, *refs):
    toks, pair_hbm, down_hbm = refs[:groups], refs[groups], refs[groups + 1]
    gate_out, up_out, pair, down, tok_all, sems = refs[groups + 3 :]
    rows, width = toks[0].shape
    steps = width // chunk
    pairs, downs = [], []
    for step in range(steps):
        at = pl.ds(step * chunk, chunk)
        pairs.append(
            pltpu.make_async_copy(pair_hbm.at[:, at, :], pair.at[:, at, :], sems.at[0, step])
        )
        downs.append(pltpu.make_async_copy(down_hbm.at[:, at], down.at[:, at], sems.at[1, step]))
    for one in pairs + downs:
        one.start()
    for group in range(groups):
        tok_all[group * rows : (group + 1) * rows, :] = toks[group][...]
    gate_out[...] = jnp.zeros_like(gate_out)
    up_out[...] = jnp.zeros_like(up_out)
    for step in range(steps):
        at = slice(step * chunk, (step + 1) * chunk)
        pairs[step].wait()
        gate_out[...] += dot_nn(tok_all[:, at], pair[0, at, :])
        up_out[...] += dot_nn(tok_all[:, at], pair[1, at, :])
    for one in downs:
        one.wait()


def forward(toks, pair, down, after):
    groups = len(toks)
    rows, width = toks[0].shape
    units = down.shape[0]
    chunk = min(512, width)
    total = groups * rows
    return pl.pallas_call(
        functools.partial(forward_kernel, groups, chunk),
        in_specs=[VMEM] * groups + [HBM] * 2 + [pl.BlockSpec(memory_space=pl.ANY)],
        out_specs=[VMEM] * 4,
        out_shape=[
            jax.ShapeDtypeStruct((total, units), jnp.float32),
            jax.ShapeDtypeStruct((total, units), jnp.float32),
            pltpu.VMEM(pair.shape, jnp.bfloat16),
            pltpu.VMEM(down.shape, jnp.bfloat16),
        ],
        scratch_shapes=[
            pltpu.VMEM((total, width), jnp.bfloat16),
            pltpu.SemaphoreType.DMA((2, width // chunk)),
        ],
        compiler_params=params(28),
        cost_estimate=cost(4 * total * width * units, 6 * width * units),
        name="forward_rows",
    )(*toks, in_hbm(pair), in_hbm(down), after)


def backward_kernel(groups, chunk, *refs):
    cots, pre_gate_ref, pre_up_ref = refs[:groups], refs[groups], refs[groups + 1]
    pair, down = refs[groups + 2 : groups + 4]
    gate_out, up_out, hidden_out = refs[groups + 4 : groups + 7]
    parts, acc = refs[groups + 7 : 2 * groups + 7], refs[2 * groups + 7]
    rows, width = cots[0].shape
    steps = width // chunk
    for step in range(steps):
        at = slice(step * chunk, (step + 1) * chunk)
        cot = jnp.concatenate([ref[:, at] for ref in cots], axis=0)
        value = dot_nt(cot, down[:, at])
        acc[...] = value if step == 0 else acc[...] + value
    pre_gate, pre_up, hidden_grad = pre_gate_ref[...], pre_up_ref[...], acc[...]
    sigmoid_gate = jax.nn.sigmoid(pre_gate)
    activated = pre_gate * sigmoid_gate
    hidden_out[...] = (activated * pre_up).astype(jnp.bfloat16)
    gate_grad = (
        hidden_grad * pre_up * sigmoid_gate * (1.0 + pre_gate * (1.0 - sigmoid_gate))
    ).astype(jnp.bfloat16)
    up_grad = (hidden_grad * activated).astype(jnp.bfloat16)
    gate_out[...] = gate_grad
    up_out[...] = up_grad
    for step in range(steps):
        at = slice(step * chunk, (step + 1) * chunk)
        value = dot_nt(gate_grad, pair[0, at, :]) + dot_nt(up_grad, pair[1, at, :])
        for group in range(groups):
            parts[group][:, at] = value[group * rows : (group + 1) * rows].astype(
                parts[group].dtype
            )


def backward(cots, pre_gate, pre_up, pair, down):
    groups = len(cots)
    rows, width = cots[0].shape
    total, units = pre_gate.shape
    chunk = min(512, width)
    out_shape = [bf16(total, units)] * 3
    out_shape += [
        jax.ShapeDtypeStruct((rows, width), jnp.float32 if group == 0 else jnp.bfloat16)
        for group in range(groups)
    ]
    out = pl.pallas_call(
        functools.partial(backward_kernel, groups, chunk),
        in_specs=[VMEM] * (groups + 4),
        out_specs=[VMEM] * len(out_shape),
        out_shape=out_shape,
        scratch_shapes=[pltpu.VMEM((total, units), jnp.float32)],
        compiler_params=params(28),
        cost_estimate=cost(6 * total * width * units, 6 * width * units),
        name="backward_rows",
    )(
        *cots,
        pre_gate,
        pre_up,
        pltpu.with_memory_space_constraint(pair, pltpu.VMEM),
        pltpu.with_memory_space_constraint(down, pltpu.VMEM),
    )
    return out[0], out[1], out[2], out[3:]


def add_parts(own, others, after):
    rows, width = own.shape
    number = rows // CAP
    count = len(others)

    def body(*refs):
        total = refs[0][...]
        for other in refs[1 : 1 + count]:
            total = total + other[...].astype(jnp.float32)
        total = total.astype(jnp.bfloat16)
        for index in range(number):
            refs[2 + count][index] = total[index * CAP : (index + 1) * CAP]

    return pl.pallas_call(
        body,
        in_specs=[VMEM] * (1 + count) + [HBM],
        out_specs=VMEM,
        out_shape=bf16(number, CAP, width),
        compiler_params=params(16),
        cost_estimate=cost(rows * width, 8 * rows * width),
        name="add_parts",
    )(own, *others, in_hbm(after))


def pair_grad_kernel(blocks, chunk, *refs):
    toks, gate_ref, up_ref = refs[:blocks], refs[blocks], refs[blocks + 1]
    out_hbm, buffer, sems = refs[blocks + 3 :]
    width = toks[0].shape[1]
    copies = []
    for step in range(width // chunk):
        at = slice(step * chunk, (step + 1) * chunk)
        tok = jnp.concatenate([ref[:, at] for ref in toks], axis=0)
        for side, ref in enumerate((gate_ref, up_ref)):
            buffer[side, at, :] = dot_tn(tok, ref[...]).astype(jnp.bfloat16)
        where = pl.ds(step * chunk, chunk)
        one = pltpu.make_async_copy(
            buffer.at[:, where, :], out_hbm.at[0, :, where, :], sems.at[step]
        )
        one.start()
        copies.append(one)
    for one in copies:
        one.wait()


def pair_grad(toks, gate_grad, up_grad, after):
    blocks = len(toks)
    width = toks[0].shape[1]
    total, units = gate_grad.shape
    chunk = min(512, width)
    return pl.pallas_call(
        functools.partial(pair_grad_kernel, blocks, chunk),
        in_specs=[VMEM] * (blocks + 2) + [pl.BlockSpec(memory_space=pl.ANY)],
        out_specs=HBM,
        out_shape=bf16(1, 2, width, units),
        scratch_shapes=[
            pltpu.VMEM((2, width, units), jnp.bfloat16),
            pltpu.SemaphoreType.DMA((width // chunk,)),
        ],
        compiler_params=params(32),
        cost_estimate=cost(4 * total * width * units, 4 * width * units),
        name="pair_grad",
    )(*toks, gate_grad, up_grad, after)


def down_grad_kernel(blocks, chunk, *refs):
    cots, hidden_ref, out_hbm = refs[:blocks], refs[blocks], refs[blocks + 1]
    buffer, sems = refs[blocks + 2 :]
    width = cots[0].shape[1]
    copies = []
    for step in range(width // chunk):
        at = slice(step * chunk, (step + 1) * chunk)
        cot = jnp.concatenate([ref[:, at] for ref in cots], axis=0)
        buffer[:, at] = dot_tn(hidden_ref[...], cot).astype(jnp.bfloat16)
        where = pl.ds(step * chunk, chunk)
        one = pltpu.make_async_copy(buffer.at[:, where], out_hbm.at[0, :, where], sems.at[step])
        one.start()
        copies.append(one)
    for one in copies:
        one.wait()


def down_grad(cots, hidden):
    blocks = len(cots)
    width = cots[0].shape[1]
    total, units = hidden.shape
    chunk = min(1024, width)
    return pl.pallas_call(
        functools.partial(down_grad_kernel, blocks, chunk),
        in_specs=[VMEM] * (blocks + 1),
        out_specs=HBM,
        out_shape=bf16(1, units, width),
        scratch_shapes=[
            pltpu.VMEM((units, width), jnp.bfloat16),
            pltpu.SemaphoreType.DMA((width // chunk,)),
        ],
        compiler_params=params(24),
        cost_estimate=cost(2 * total * width * units, 2 * width * units),
        name="down_grad",
    )(*cots, hidden)


def spread_kernel(chunk, rows_ref, place_ref, out_hbm, buffer, sems):
    number, _, width = rows_ref.shape
    place = place_ref[...]
    copies = []
    for step in range(width // chunk):
        at = slice(step * chunk, (step + 1) * chunk)
        rows = jnp.concatenate([rows_ref[index, :, at] for index in range(number)], axis=0)
        buffer[:, at] = dot_tn(place, rows).astype(jnp.bfloat16)
        where = pl.ds(step * chunk, chunk)
        one = pltpu.make_async_copy(buffer.at[:, where], out_hbm.at[:, where], sems.at[step])
        one.start()
        copies.append(one)
    for one in copies:
        one.wait()


def spread(rows, place):
    number, _, width = rows.shape
    tokens = place.shape[1]
    chunk = min(1024, width)
    return pl.pallas_call(
        functools.partial(spread_kernel, chunk),
        in_specs=[VMEM] * 2,
        out_specs=HBM,
        out_shape=bf16(tokens, width),
        scratch_shapes=[
            pltpu.VMEM((tokens, width), jnp.bfloat16),
            pltpu.SemaphoreType.DMA((width // chunk,)),
        ],
        compiler_params=params(16),
        cost_estimate=cost(2 * number * CAP * tokens * width, 2 * tokens * width),
        name="spread_rows",
    )(rows, place)


def per_device(activations, cotangent, expert_ids, gate_probs, gate_up, down_proj):
    experts = lax.axis_size("expert")
    groups = lax.axis_size("dp")
    tokens, width = activations.shape

    def exchange(value):
        return lax.all_to_all(value, "expert", split_axis=0, concat_axis=0, tiled=True)

    def shift(value, by):
        return lax.ppermute(value, "dp", [(i, (i + by) % groups) for i in range(groups)])

    send_tok, send_cot, place = route(
        expert_ids.reshape(1, tokens), gate_probs.reshape(1, tokens), activations, cotangent, experts
    )
    own_tok = exchange(send_tok).reshape(experts * CAP, width)
    toks = [own_tok] + [shift(own_tok, by) for by in range(1, groups)]
    own_cot = exchange(send_cot).reshape(experts * CAP, width)
    cots = [own_cot] + [shift(own_cot, by) for by in range(1, groups)]
    pre_gate, pre_up, pair, down = forward(toks, gate_up[0], down_proj[0], own_cot)
    gate_grad, up_grad, hidden, parts = backward(cots, pre_gate, pre_up, pair, down)
    others = [shift(parts[by], -by) for by in range(1, groups)]
    down_total = down_grad(cots, hidden)
    rounded = add_parts(parts[0], others, down_total)
    returned = exchange(rounded)
    pair_total = pair_grad(toks, gate_grad, up_grad, rounded)
    input_grad = spread(returned, place)
    return input_grad, pair_total, down_total


def solution(mesh):
    rows = P(("dp", "expert"), None)
    pair, down = P("expert", None, None, "dp"), P("expert", "dp", None)
    return jax.shard_map(
        per_device,
        mesh=mesh,
        in_specs=(rows, rows, rows, rows, pair, down),
        out_specs=(rows, pair, down),
        check_vma=False,
    )
```

profile of v0, /device:TPU:0, one launch (start us, length us, event | category | flops | bytes accessed | tf_op | source)
XLA Modules:
  0.0 72.7 jit_solution(3958666664294529295)
XLA Ops:
  0.6 2.7 %route_rows.1 = (bf16[16,2,4096]{2,1,0:T(2,128)(2,1)S(1)}, bf16[16,2,4096]{2,1,0:T(2,128)(2,1)}, bf16[32,128]{1,0:T(8,128)(2,1)S(1)}) custom-call(s32[1,128]{1,0:T(1,128)} %bitcast.6, f32[1,128]{1,0:T(1,128)} %bitcast.7, bf16[128,4096]{1,0:T(8,128)(2,1)} %act_hbm.1, bf16[128,4096]{1,0:T(8,128)(2,1)} %cot_hbm.1), custom_call_target="tpu_custom_call" | custom-call | flops 67108864 | bytes 2097152 | tf_op jit(solution)/shard_map/route_rows/pallas_call | solution.py:98
  3.4 17.2 %all_to_all.15 = bf16[16,2,4096]{2,1,0:T(2,128)(2,1)S(1)} all-to-all(bf16[16,2,4096]{2,1,0:T(2,128)(2,1)S(1)} %get-tuple-element.16), channel_id=1, replica_groups=mesh['dp'=2,'expert'=16] {'expert'}, dimensions={0} | all-to-all | bytes 524288 | tf_op jit(solution)/shard_map/all_to_all | solution.py:371
  20.6 3.5 %all-to-all-start = ((bf16[16,2,4096]{2,1,0:T(2,128)(2,1)}), bf16[16,2,4096]{2,1,0:T(2,128)(2,1)S(1)}, u32[]{:S(2)}, u32[]{:S(2)}) async-start(bf16[16,2,4096]{2,1,0:T(2,128)(2,1)} %get-tuple-element.15), calls=%async_computation | async-start | bytes 524288 | tf_op jit(solution)/shard_map/all_to_all | solution.py:371
  24.1 0.1 reshape.21.refs_0_
  24.2 1.6 %collective-permute-start.1 = (bf16[32,4096]{1,0:T(8,128)(2,1)S(1)}, bf16[32,4096]{1,0:T(8,128)(2,1)S(1)}, u32[]{:S(2)}, u32[]{:S(2)}) collective-permute-start(bf16[32,4096]{1,0:T(8,128)(2,1)S(1)} %reshape.21.refs_0_), channel_id=1, source_target_pairs={{0,16},{16,0},{1,17},{17,1},{2,18},{18,2},{3,19},{19,3},{4,20},{20... | collective-permute-start | bytes 786440 | tf_op jit(solution)/shard_map/ppermute | solution.py:374
  25.8 8.3 %all-to-all-done = bf16[16,2,4096]{2,1,0:T(2,128)(2,1)S(1)} async-done(((bf16[16,2,4096]{2,1,0:T(2,128)(2,1)}), bf16[16,2,4096]{2,1,0:T(2,128)(2,1)S(1)}, u32[]{:S(2)}, u32[]{:S(2)}) %all-to-all-start) | async-done | bytes 262176 | tf_op jit(solution)/shard_map/all_to_all | solution.py:371
  34.1 0.1 reshape.20.refs_4_.refs_0_
  34.2 1.6 %collective-permute-start = (bf16[32,4096]{1,0:T(8,128)(2,1)S(1)}, bf16[32,4096]{1,0:T(8,128)(2,1)S(1)}, u32[]{:S(2)}, u32[]{:S(2)}) collective-permute-start(bf16[32,4096]{1,0:T(8,128)(2,1)S(1)} %reshape.20.refs_4_.refs_0_), channel_id=1, source_target_pairs={{0,16},{16,0},{1,17},{17,1},{2,18},{18,2},{3,19},{19,3},{4,20},{20... | collective-permute-start | bytes 786440 | tf_op jit(solution)/shard_map/ppermute | solution.py:374
  35.8 0.0 collective-permute-done.1.refs_1_
  35.8 6.6 %forward_rows.1 = (f32[64,768]{1,0:T(8,128)S(1)}, f32[64,768]{1,0:T(8,128)S(1)}, bf16[2,4096,768]{2,1,0:T(8,128)(2,1)S(1)}, bf16[768,4096]{1,0:T(8,128)(2,1)S(1)}) custom-call(bf16[32,4096]{1,0:T(8,128)(2,1)S(1)} %reshape.21.refs_0_, bf16[32,4096]{1,0:T(8,128)(2,1)S(1)} %collective-permute-done.1.refs_1_, bf16[2,4096,768]{2,1,0:T(8,128)(2,1)} %bitcast.4, ...), custom_call_target="tpu_custom_call" | custom-call | flops 805306368 | bytes 18874368 | tf_op jit(solution)/shard_map/forward_rows/pallas_call | solution.py:149
  42.4 0.0 collective-permute-done.refs_1_
  42.4 6.8 %backward_rows.1 = (bf16[64,768]{1,0:T(8,128)(2,1)S(1)}, bf16[64,768]{1,0:T(8,128)(2,1)S(1)}, bf16[64,768]{1,0:T(8,128)(2,1)S(1)}, f32[32,4096]{1,0:T(8,128)S(1)}, bf16[32,4096]{1,0:T(8,128)(2,1)S(1)}) custom-call(bf16[32,4096]{1,0:T(8,128)(2,1)S(1)} %reshape.20.refs_4_.refs_0_, bf16[32,4096]{1,0:T(8,128)(2,1)S(1)} %collective-permute-done.refs_1_, ...), custom_call_target="tpu_custom_call" | custom-call | flops 1207959552 | bytes 18874368 | tf_op jit(solution)/shard_map/backward_rows/pallas_call | solution.py:210
  49.2 1.5 %collective-permute-start.2 = (bf16[32,4096]{1,0:T(8,128)(2,1)S(1)}, bf16[32,4096]{1,0:T(8,128)(2,1)S(1)}, u32[]{:S(2)}, u32[]{:S(2)}) collective-permute-start(bf16[32,4096]{1,0:T(8,128)(2,1)S(1)} %get-tuple-element.22), channel_id=1, source_target_pairs={{0,16},{16,0},{1,17},{17,1},{2,18},{18,2},{3,19},{19,3},{4,20},{20... | collective-permute-start | bytes 786440 | tf_op jit(solution)/shard_map/ppermute | solution.py:374
  50.7 3.3 %down_grad.1.refs_2_ = bf16[1,768,4096]{2,1,0:T(8,128)(2,1)} custom-call(bf16[32,4096]{1,0:T(8,128)(2,1)S(1)} %reshape.20.refs_4_.refs_0_, bf16[32,4096]{1,0:T(8,128)(2,1)S(1)} %collective-permute-done.refs_1_, bf16[64,768]{1,0:T(8,128)(2,1)S(1)} %get-tuple-element.23.refs_2_), custom_call_target="tpu_custom_call" | custom-call | flops 402653184 | bytes 6291456 | tf_op jit(solution)/shard_map/down_grad/pallas_call | solution.py:315
  54.0 3.0 %collective-permute-done.2.refs_1_ = bf16[32,4096]{1,0:T(8,128)(2,1)S(1)} collective-permute-done((bf16[32,4096]{1,0:T(8,128)(2,1)S(1)}, bf16[32,4096]{1,0:T(8,128)(2,1)S(1)}, u32[]{:S(2)}, u32[]{:S(2)}) %collective-permute-start.2) | collective-permute-done | bytes 262176 | tf_op jit(solution)/shard_map/ppermute | solution.py:374
  57.0 0.8 %add_parts.1.refs_4_ = bf16[16,2,4096]{2,1,0:T(2,128)(2,1)} custom-call(f32[32,4096]{1,0:T(8,128)S(1)} %get-tuple-element.21.refs_0_, bf16[32,4096]{1,0:T(8,128)(2,1)S(1)} %collective-permute-done.2.refs_1_, bf16[1,768,4096]{2,1,0:T(8,128)(2,1)} %down_grad.1.refs_2_), custom_call_target="tpu_custom_call" | custom-call | flops 131072 | bytes 1048576 | tf_op jit(solution)/shard_map/add_parts/pallas_call | solution.py:242
  57.8 3.7 %all-to-all-start.2 = ((bf16[16,2,4096]{2,1,0:T(2,128)(2,1)}), bf16[16,2,4096]{2,1,0:T(2,128)(2,1)S(1)}, u32[]{:S(2)}, u32[]{:S(2)}) async-start(bf16[16,2,4096]{2,1,0:T(2,128)(2,1)} %add_parts.1.refs_4_), calls=%async_computation.2 | async-start | bytes 524288 | tf_op jit(solution)/shard_map/all_to_all | solution.py:371
  61.5 5.2 %pair_grad.1 = bf16[1,2,4096,768]{3,2,1,0:T(8,128)(2,1)} custom-call(bf16[32,4096]{1,0:T(8,128)(2,1)S(1)} %reshape.21.refs_0_, bf16[32,4096]{1,0:T(8,128)(2,1)S(1)} %collective-permute-done.1.refs_1_, bf16[64,768]{1,0:T(8,128)(2,1)S(1)} %get-tuple-element.25.refs_2_, bf16[64,768]{1,0:T(8,128)(2,1)S(1)} %get-tuple-element.26.refs_3_, ...), custom_call_target="tpu_custom_call" | custom-call | flops 805306368 | bytes 12582912 | tf_op jit(solution)/shard_map/pair_grad/pallas_call | solution.py:278
  66.8 4.6 %all-to-all-done.2.rows_ref = bf16[16,2,4096]{2,1,0:T(2,128)(2,1)S(1)} async-done(((bf16[16,2,4096]{2,1,0:T(2,128)(2,1)}), bf16[16,2,4096]{2,1,0:T(2,128)(2,1)S(1)}, u32[]{:S(2)}, u32[]{:S(2)}) %all-to-all-start.2) | async-done | bytes 262176 | tf_op jit(solution)/shard_map/all_to_all | solution.py:371
  71.3 1.3 %spread_rows.1 = bf16[128,4096]{1,0:T(8,128)(2,1)} custom-call(bf16[16,2,4096]{2,1,0:T(2,128)(2,1)S(1)} %all-to-all-done.2.rows_ref, bf16[32,128]{1,0:T(8,128)(2,1)S(1)} %get-tuple-element.24.place_ref), custom_call_target="tpu_custom_call" | custom-call | flops 33554432 | bytes 1048576 | tf_op jit(solution)/shard_map/spread_rows/pallas_call | solution.py:350
Async XLA Ops:
  20.6 13.5 %all-to-all-start = ((bf16[16,2,4096]{2,1,0:T(2,128)(2,1)}), bf16[16,2,4096]{2,1,0:T(2,128)(2,1)S(1)}, u32[]{:S(2)}, u32[]{:S(2)}) async-start(bf16[16,2,4096]{2,1,0:T(2,128)(2,1)} %get-tuple-element.15), calls=%async_computation | async-start | bytes 524288 | tf_op jit(solution)/shard_map/all_to_all | solution.py:371
  24.2 11.6 %collective-permute-start.1 = (bf16[32,4096]{1,0:T(8,128)(2,1)S(1)}, bf16[32,4096]{1,0:T(8,128)(2,1)S(1)}, u32[]{:S(2)}, u32[]{:S(2)}) collective-permute-start(bf16[32,4096]{1,0:T(8,128)(2,1)S(1)} %reshape.21.refs_0_), channel_id=1, source_target_pairs={{0,16},{16,0},{1,17},{17,1},{2,18},{18,2},{3,19},{19,3},{4,20},{20... | collective-permute-start | bytes 786440 | tf_op jit(solution)/shard_map/ppermute | solution.py:374
  34.2 8.2 %collective-permute-start = (bf16[32,4096]{1,0:T(8,128)(2,1)S(1)}, bf16[32,4096]{1,0:T(8,128)(2,1)S(1)}, u32[]{:S(2)}, u32[]{:S(2)}) collective-permute-start(bf16[32,4096]{1,0:T(8,128)(2,1)S(1)} %reshape.20.refs_4_.refs_0_), channel_id=1, source_target_pairs={{0,16},{16,0},{1,17},{17,1},{2,18},{18,2},{3,19},{19,3},{4,20},{20... | collective-permute-start | bytes 786440 | tf_op jit(solution)/shard_map/ppermute | solution.py:374
  49.2 7.8 %collective-permute-start.2 = (bf16[32,4096]{1,0:T(8,128)(2,1)S(1)}, bf16[32,4096]{1,0:T(8,128)(2,1)S(1)}, u32[]{:S(2)}, u32[]{:S(2)}) collective-permute-start(bf16[32,4096]{1,0:T(8,128)(2,1)S(1)} %get-tuple-element.22), channel_id=1, source_target_pairs={{0,16},{16,0},{1,17},{17,1},{2,18},{18,2},{3,19},{19,3},{4,20},{20... | collective-permute-start | bytes 786440 | tf_op jit(solution)/shard_map/ppermute | solution.py:374
  57.8 13.5 %all-to-all-start.2 = ((bf16[16,2,4096]{2,1,0:T(2,128)(2,1)}), bf16[16,2,4096]{2,1,0:T(2,128)(2,1)S(1)}, u32[]{:S(2)}, u32[]{:S(2)}) async-start(bf16[16,2,4096]{2,1,0:T(2,128)(2,1)} %add_parts.1.refs_4_), calls=%async_computation.2 | async-start | bytes 524288 | tf_op jit(solution)/shard_map/all_to_all | solution.py:371
where the time goes:
time: 73.2 us; the launch traced here: 72.7 us
  Pallas kernels  26.7 us (36%)
  blocking collectives  17.2 us (23%)
  waiting for transfers between devices  15.9 us (22%)
  starting transfers between devices  11.9 us (16%)
  between operations  0.87 us (1%)
    all_to_all x1, blocking collectives, exchange(): lax.all_to_all(value, 'expert', split_axis=0, concat_axis=0, tiled=True)  17.2 us
    all_to_all x2, waiting for transfers between devices, exchange(): lax.all_to_all(value, 'expert', split_axis=0, concat_axis=0, tiled=True)  12.9 us
    all_to_all x2, starting transfers between devices, exchange(): lax.all_to_all(value, 'expert', split_axis=0, concat_axis=0, tiled=True)  7.25 us
    pallas_call x1, Pallas kernels, backward(): pl.pallas_call(functools.partial(backward_kernel, groups, chunk), in_spec...  6.75 us
    pallas_call x1, Pallas kernels, forward(): pl.pallas_call(functools.partial(forward_kernel, groups, chunk), in_specs...  6.57 us
    pallas_call x1, Pallas kernels, pair_grad(): pl.pallas_call(functools.partial(pair_grad_kernel, blocks, chunk), in_spe...  5.25 us
    ppermute x3, starting transfers between devices, shift(): lax.ppermute(value, 'dp', [(i, (i + by) % groups) for i in range(groups)])  4.68 us
    pallas_call x1, Pallas kernels, down_grad(): pl.pallas_call(functools.partial(down_grad_kernel, blocks, chunk), in_spe...  3.32 us
  transfers between devices with their start and end apart: 5, of which 3 were waited for; matrix products, arithmetic and copies ran while one was open for 0% of the time, Pallas kernels for 21%

commit v1 on v0

v1 whole, which is shorter than its diff:
```python
import functools

import jax
import jax.numpy as jnp
from jax import lax
from jax.experimental import pallas as pl
from jax.experimental.pallas import tpu as pltpu
from jax.sharding import PartitionSpec as P

CAP = 2
MIB = 1024 * 1024
VMEM = pl.BlockSpec(memory_space=pltpu.VMEM)
HBM = pl.BlockSpec(memory_space=pltpu.HBM)


def dot_nn(a, b):
    return lax.dot_general(a, b, (((1,), (0,)), ((), ())), preferred_element_type=jnp.float32)


def dot_nt(a, b):
    return lax.dot_general(a, b, (((1,), (1,)), ((), ())), preferred_element_type=jnp.float32)


def dot_tn(a, b):
    return lax.dot_general(a, b, (((0,), (0,)), ((), ())), preferred_element_type=jnp.float32)


def cost(flops, moved):
    return pl.CostEstimate(flops=int(flops), bytes_accessed=int(moved), transcendentals=0)


def params(mib):
    return pltpu.CompilerParams(vmem_limit_bytes=mib * MIB)


def in_hbm(value):
    return pltpu.with_memory_space_constraint(value, pltpu.HBM)


def bf16(*shape):
    return jax.ShapeDtypeStruct(shape, jnp.bfloat16)


def route_kernel(experts, groups, chunk, ids_hbm, probs_hbm, act_hbm, cot_hbm, *refs):
    send_hbm, place_ref, ids_ref, probs_ref, act, cot, send, sems, out_sems = refs
    tokens, width = act.shape
    steps = width // chunk
    small = (
        pltpu.make_async_copy(ids_hbm, ids_ref, sems.at[2 * steps]),
        pltpu.make_async_copy(probs_hbm, probs_ref, sems.at[2 * steps + 1]),
    )
    large = []
    for step in range(steps):
        at = pl.ds(step * chunk, chunk)
        large.append(
            (
                pltpu.make_async_copy(act_hbm.at[:, at], act.at[:, at], sems.at[2 * step]),
                pltpu.make_async_copy(cot_hbm.at[:, at], cot.at[:, at], sems.at[2 * step + 1]),
            )
        )
    for one in small:
        one.start()
    for pair in large:
        for one in pair:
            one.start()
    for one in small:
        one.wait()

    ids = ids_ref[...]
    inside = ids < experts
    near = jnp.where(inside, ids, -CAP)
    units = lax.broadcasted_iota(jnp.int32, (experts, tokens), 0)
    onehot = jnp.where(units == near, 1.0, 0.0)
    earlier = lax.broadcasted_iota(jnp.int32, (tokens, tokens), 0) < lax.broadcasted_iota(
        jnp.int32, (tokens, tokens), 1
    )
    before = dot_nn(onehot.astype(jnp.bfloat16), jnp.where(earlier, 1.0, 0.0).astype(jnp.bfloat16))
    rank = jnp.sum(before * onehot, axis=0, keepdims=True).astype(jnp.int32)
    slots = lax.broadcasted_iota(jnp.int32, (experts * CAP, tokens), 0)
    place = jnp.where(slots == near * CAP + rank, 1.0, 0.0)
    weight = jnp.sum(place * probs_ref[...], axis=1, keepdims=True)
    place = place.astype(jnp.bfloat16)
    place_ref[...] = place
    sent = []
    for step in range(steps):
        at = slice(step * chunk, (step + 1) * chunk)
        for one in large[step]:
            one.wait()
        rows_tok = dot_nn(place, act[:, at]).astype(jnp.bfloat16)
        rows_cot = (weight * dot_nn(place, cot[:, at])).astype(jnp.bfloat16)
        for unit in range(experts):
            send[unit, :CAP, at] = rows_tok[unit * CAP : (unit + 1) * CAP]
            send[unit, CAP:, at] = rows_cot[unit * CAP : (unit + 1) * CAP]
        where = pl.ds(step * chunk, chunk)
        for group in range(groups):
            block = pl.ds(group * experts, experts)
            one = pltpu.make_async_copy(
                send.at[:, :, where], send_hbm.at[block, :, where], out_sems.at[group, step]
            )
            one.start()
            sent.append(one)
    for one in sent:
        one.wait()


def route(ids, probs, act, cot, experts, groups):
    tokens, width = act.shape
    chunk = min(1024, width)
    return pl.pallas_call(
        functools.partial(route_kernel, experts, groups, chunk),
        in_specs=[HBM] * 4,
        out_specs=[HBM, VMEM],
        out_shape=[
            pltpu.HBM((groups * experts, 2 * CAP, width), jnp.bfloat16),
            bf16(experts * CAP, tokens),
        ],
        scratch_shapes=[
            pltpu.VMEM((1, tokens), jnp.int32),
            pltpu.VMEM((1, tokens), jnp.float32),
            pltpu.VMEM((tokens, width), jnp.bfloat16),
            pltpu.VMEM((tokens, width), jnp.bfloat16),
            pltpu.VMEM((experts, 2 * CAP, width), jnp.bfloat16),
            pltpu.SemaphoreType.DMA((2 * (width // chunk) + 2,)),
            pltpu.SemaphoreType.DMA((groups, width // chunk)),
        ],
        compiler_params=params(16),
        cost_estimate=cost(4 * experts * CAP * tokens * width, 4 * tokens * width),
        name="route_rows",
    )(in_hbm(ids), in_hbm(probs), in_hbm(act), in_hbm(cot))


def load_kernel(chunk, pair_hbm, down_hbm, after, pair, down, sems):
    del after
    width = down.shape[1]
    copies = []
    for step in range(width // chunk):
        at = pl.ds(step * chunk, chunk)
        copies += [
            pltpu.make_async_copy(pair_hbm.at[:, at, :], pair.at[:, at, :], sems.at[0, step]),
            pltpu.make_async_copy(down_hbm.at[:, at], down.at[:, at], sems.at[1, step]),
        ]
    for one in copies:
        one.start()
    for one in copies:
        one.wait()


def load(pair, down, after):
    units, width = down.shape
    chunk = min(1024, width)
    return pl.pallas_call(
        functools.partial(load_kernel, chunk),
        in_specs=[HBM] * 2 + [pl.BlockSpec(memory_space=pl.ANY)],
        out_specs=[VMEM] * 2,
        out_shape=[pltpu.VMEM(pair.shape, jnp.bfloat16), pltpu.VMEM(down.shape, jnp.bfloat16)],
        scratch_shapes=[pltpu.SemaphoreType.DMA((2, width // chunk))],
        compiler_params=params(28),
        cost_estimate=cost(0, 6 * width * units),
        name="load_weights",
    )(in_hbm(pair), in_hbm(down), after)


def expert_kernel(chunk, got, pair, down, *refs):
    gate_out, up_out, hidden_out, tok_all, cot_all, parts_hbm = refs[:6]
    parts, acc_gate, acc_up, acc_hid, sems = refs[6:]
    blocks, _, width = got.shape
    steps = width // chunk
    for step in range(steps):
        at = slice(step * chunk, (step + 1) * chunk)
        tok = jnp.concatenate([got[block, :CAP, at] for block in range(blocks)], axis=0)
        cot = jnp.concatenate([got[block, CAP:, at] for block in range(blocks)], axis=0)
        tok_all[:, at] = tok
        cot_all[:, at] = cot
        gate = dot_nn(tok, pair[0, at, :])
        up = dot_nn(tok, pair[1, at, :])
        hid = dot_nt(cot, down[:, at])
        if step == 0:
            acc_gate[...], acc_up[...], acc_hid[...] = gate, up, hid
        else:
            acc_gate[...] += gate
            acc_up[...] += up
            acc_hid[...] += hid
    pre_gate, pre_up, hidden_grad = acc_gate[...], acc_up[...], acc_hid[...]
    sigmoid_gate = jax.nn.sigmoid(pre_gate)
    activated = pre_gate * sigmoid_gate
    hidden_out[...] = (activated * pre_up).astype(jnp.bfloat16)
    gate_grad = (
        hidden_grad * pre_up * sigmoid_gate * (1.0 + pre_gate * (1.0 - sigmoid_gate))
    ).astype(jnp.bfloat16)
    up_grad = (hidden_grad * activated).astype(jnp.bfloat16)
    gate_out[...] = gate_grad
    up_out[...] = up_grad
    copies = []
    for step in range(steps):
        at = slice(step * chunk, (step + 1) * chunk)
        value = dot_nt(gate_grad, pair[0, at, :]) + dot_nt(up_grad, pair[1, at, :])
        value = value.astype(jnp.bfloat16)
        for block in range(blocks):
            parts[block, :, at] = value[block * CAP : (block + 1) * CAP]
        where = pl.ds(step * chunk, chunk)
        one = pltpu.make_async_copy(
            parts.at[:, :, where], parts_hbm.at[:, :, where], sems.at[step]
        )
        one.start()
        copies.append(one)
    for one in copies:
        one.wait()


def expert_rows(got, pair, down):
    blocks, _, width = got.shape
    units = down.shape[0]
    chunk = min(512, width)
    total = blocks * CAP
    return pl.pallas_call(
        functools.partial(expert_kernel, chunk),
        in_specs=[VMEM] * 3,
        out_specs=[VMEM] * 5 + [HBM],
        out_shape=[bf16(total, units)] * 3
        + [bf16(total, width)] * 2
        + [pltpu.HBM((blocks, CAP, width), jnp.bfloat16)],
        scratch_shapes=[
            pltpu.VMEM((blocks, CAP, width), jnp.bfloat16),
            pltpu.VMEM((total, units), jnp.float32),
            pltpu.VMEM((total, units), jnp.float32),
            pltpu.VMEM((total, units), jnp.float32),
            pltpu.SemaphoreType.DMA((width // chunk,)),
        ],
        compiler_params=params(28),
        cost_estimate=cost(10 * total * width * units, 6 * width * units),
        name="expert_rows",
    )(
        got,
        pltpu.with_memory_space_constraint(pair, pltpu.VMEM),
        pltpu.with_memory_space_constraint(down, pltpu.VMEM),
    )


def pair_grad_kernel(blocks, chunk, *refs):
    toks, gate_ref, up_ref = refs[:blocks], refs[blocks], refs[blocks + 1]
    out_hbm, buffer, sems = refs[blocks + 2 :]
    width = toks[0].shape[1]
    copies = []
    for step in range(width // chunk):
        at = slice(step * chunk, (step + 1) * chunk)
        tok = jnp.concatenate([ref[:, at] for ref in toks], axis=0)
        for side, ref in enumerate((gate_ref, up_ref)):
            buffer[side, at, :] = dot_tn(tok, ref[...]).astype(jnp.bfloat16)
        where = pl.ds(step * chunk, chunk)
        one = pltpu.make_async_copy(
            buffer.at[:, where, :], out_hbm.at[0, :, where, :], sems.at[step]
        )
        one.start()
        copies.append(one)
    for one in copies:
        one.wait()


def pair_grad(toks, gate_grad, up_grad):
    blocks = len(toks)
    width = toks[0].shape[1]
    total, units = gate_grad.shape
    chunk = min(512, width)
    return pl.pallas_call(
        functools.partial(pair_grad_kernel, blocks, chunk),
        in_specs=[VMEM] * (blocks + 2),
        out_specs=HBM,
        out_shape=bf16(1, 2, width, units),
        scratch_shapes=[
            pltpu.VMEM((2, width, units), jnp.bfloat16),
            pltpu.SemaphoreType.DMA((width // chunk,)),
        ],
        compiler_params=params(32),
        cost_estimate=cost(4 * total * width * units, 4 * width * units),
        name="pair_grad",
    )(*toks, gate_grad, up_grad)


def down_grad_kernel(blocks, chunk, *refs):
    cots, hidden_ref, out_hbm = refs[:blocks], refs[blocks], refs[blocks + 1]
    buffer, sems = refs[blocks + 2 :]
    width = cots[0].shape[1]
    copies = []
    for step in range(width // chunk):
        at = slice(step * chunk, (step + 1) * chunk)
        cot = jnp.concatenate([ref[:, at] for ref in cots], axis=0)
        buffer[:, at] = dot_tn(hidden_ref[...], cot).astype(jnp.bfloat16)
        where = pl.ds(step * chunk, chunk)
        one = pltpu.make_async_copy(buffer.at[:, where], out_hbm.at[0, :, where], sems.at[step])
        one.start()
        copies.append(one)
    for one in copies:
        one.wait()


def down_grad(cots, hidden):
    blocks = len(cots)
    width = cots[0].shape[1]
    total, units = hidden.shape
    chunk = min(1024, width)
    return pl.pallas_call(
        functools.partial(down_grad_kernel, blocks, chunk),
        in_specs=[VMEM] * (blocks + 1),
        out_specs=HBM,
        out_shape=bf16(1, units, width),
        scratch_shapes=[
            pltpu.VMEM((units, width), jnp.bfloat16),
            pltpu.SemaphoreType.DMA((width // chunk,)),
        ],
        compiler_params=params(24),
        cost_estimate=cost(2 * total * width * units, 2 * width * units),
        name="down_grad",
    )(*cots, hidden)


def spread_kernel(chunk, rows_ref, place_ref, out_hbm, buffer, sems):
    blocks, _, width = rows_ref.shape
    place = place_ref[...]
    number = place.shape[0] // CAP
    copies = []
    for step in range(width // chunk):
        at = slice(step * chunk, (step + 1) * chunk)
        total = 0.0
        for start in range(0, blocks, number):
            part = [rows_ref[start + index, :, at] for index in range(number)]
            total = total + jnp.concatenate(part, axis=0).astype(jnp.float32)
        buffer[:, at] = dot_tn(place, total.astype(jnp.bfloat16)).astype(jnp.bfloat16)
        where = pl.ds(step * chunk, chunk)
        one = pltpu.make_async_copy(buffer.at[:, where], out_hbm.at[:, where], sems.at[step])
        one.start()
        copies.append(one)
    for one in copies:
        one.wait()


def spread(rows, place):
    width = rows.shape[2]
    slots, tokens = place.shape
    chunk = min(1024, width)
    return pl.pallas_call(
        functools.partial(spread_kernel, chunk),
        in_specs=[VMEM] * 2,
        out_specs=HBM,
        out_shape=bf16(tokens, width),
        scratch_shapes=[
            pltpu.VMEM((tokens, width), jnp.bfloat16),
            pltpu.SemaphoreType.DMA((width // chunk,)),
        ],
        compiler_params=params(16),
        cost_estimate=cost(2 * slots * tokens * width, 2 * tokens * width),
        name="spread_rows",
    )(rows, place)


def per_device(activations, cotangent, expert_ids, gate_probs, gate_up, down_proj):
    experts = lax.axis_size("expert")
    groups = lax.axis_size("dp")
    tokens = activations.shape[0]

    def exchange(value):
        return lax.all_to_all(value, ("dp", "expert"), split_axis=0, concat_axis=0, tiled=True)

    send, place = route(
        expert_ids.reshape(1, tokens),
        gate_probs.reshape(1, tokens),
        activations,
        cotangent,
        experts,
        groups,
    )
    got = exchange(send)
    pair, down = load(gate_up[0], down_proj[0], place)
    gate_grad, up_grad, hidden, tok, cot, parts = expert_rows(got, pair, down)
    returned = exchange(parts)
    down_total = down_grad([cot], hidden)
    pair_total = pair_grad([tok], gate_grad, up_grad)
    input_grad = spread(returned, place)
    return input_grad, pair_total, down_total


def solution(mesh):
    rows = P(("dp", "expert"), None)
    pair, down = P("expert", None, None, "dp"), P("expert", "dp", None)
    return jax.shard_map(
        per_device,
        mesh=mesh,
        in_specs=(rows, rows, rows, rows, pair, down),
        out_specs=(rows, pair, down),
        check_vma=False,
    )
```

time: 73.2 us -> 75.4 us (1.030)
  blocking collectives: 17.2 us -> 0 us
  local copies, waits for them, and re-layouts: 0.2 us -> 14.8 us
  waiting for transfers between devices: 15.9 us -> 20.5 us
  Pallas kernels: 26.7 us -> 29.1 us
  starting transfers between devices: 11.9 us -> 9.93 us
    all_to_all x1 -> x0, blocking collectives: 17.2 us -> none  [exchange(): lax.all_to_all(value, 'expert', split_axis=0, concat_axis=0, tiled=True)]
    unnamed x0 -> x8, local copies, waits for them, and re-layouts: none -> 14.8 us
    all_to_all x2, waiting for transfers between devices: 12.9 us -> 20.5 us  [exchange(): lax.all_to_all(value, ('dp', 'expert'), split_axis=0, concat_axis=0, tile...]
    ppermute x3 -> x0, starting transfers between devices: 4.68 us -> none  [shift(): lax.ppermute(value, 'dp', [(i, (i + by) % groups) for i in range(groups)])]
    ppermute x3 -> x0, waiting for transfers between devices: 2.99 us -> none  [shift(): lax.ppermute(value, 'dp', [(i, (i + by) % groups) for i in range(groups)])]
    all_to_all x2, starting transfers between devices: 7.25 us -> 9.93 us  [exchange(): lax.all_to_all(value, ('dp', 'expert'), split_axis=0, concat_axis=0, tile...]
    pallas_call x4 -> x3, Pallas kernels: 16.8 us -> 19 us  [the longest x1 9.74 us: expert_rows(): pl.pallas_call(functools.partial(expert_kernel, chunk), in_specs=[VMEM] *...]
  transfers between devices with their start and end apart: 5 -> 2, of which waited for: 3 -> 2; matrix products, arithmetic and copies ran while one was open for 0% -> 0% of each run, Pallas kernels for 21% -> 20%
where the time goes in v1:
time: 75.4 us; the launch traced here: 75 us
  Pallas kernels  29.1 us (39%)
  waiting for transfers between devices  20.5 us (27%)
  local copies, waits for them, and re-layouts  14.8 us (20%)
  starting transfers between devices  9.93 us (13%)
    all_to_all x2, waiting for transfers between devices, exchange(): lax.all_to_all(value, ('dp', 'expert'), split_axis=0, concat_axis=0, tile...  20.5 us
    unnamed x8, local copies, waits for them, and re-layouts  14.8 us
    all_to_all x2, starting transfers between devices, exchange(): lax.all_to_all(value, ('dp', 'expert'), split_axis=0, concat_axis=0, tile...  9.93 us
    pallas_call x1, Pallas kernels, expert_rows(): pl.pallas_call(functools.partial(expert_kernel, chunk), in_specs=[VMEM] *...  9.74 us
    pallas_call x1, Pallas kernels, load(): pl.pallas_call(functools.partial(load_kernel, chunk), in_specs=[HBM] * 2...  6.5 us
    pallas_call x1, Pallas kernels, pair_grad(): pl.pallas_call(functools.partial(pair_grad_kernel, blocks, chunk), in_spe...  5.26 us
    pallas_call x1, Pallas kernels, down_grad(): pl.pallas_call(functools.partial(down_grad_kernel, blocks, chunk), in_spe...  3.32 us
    pallas_call x1, Pallas kernels, route(): pl.pallas_call(functools.partial(route_kernel, experts, groups, chunk), i...  2.79 us
  transfers between devices with their start and end apart: 2, of which 2 were waited for; matrix products, arithmetic and copies ran while one was open for 0% of the time, Pallas kernels for 20%

profile of v1, /device:TPU:0, one launch (start us, length us, event | category | flops | bytes accessed | tf_op | source)
XLA Modules:
  0.0 75.0 jit_solution(13759408391664337256)
XLA Ops:
  0.6 2.8 %route_rows.1 = (bf16[32,4,4096]{2,1,0:T(4,128)(2,1)}, bf16[32,128]{1,0:T(8,128)(2,1)S(1)}) custom-call(s32[1,128]{1,0:T(1,128)} %bitcast.6, f32[1,128]{1,0:T(1,128)} %bitcast.7, bf16[128,4096]{1,0:T(8,128)(2,1)} %act_hbm.1, bf16[128,4096]{1,0:T(8,128)(2,1)} %cot_hbm.1), custom_call_target="tpu_custom_call" | custom-call | flops 67108864 | bytes 2097152 | tf_op jit(solution)/shard_map/route_rows/pallas_call | solution.py:109
  3.4 7.3 %all-to-all-start = ((bf16[32,4,4096]{2,1,0:T(4,128)(2,1)}), bf16[32,4,4096]{2,1,0:T(4,128)(2,1)S(1)}, u32[]{:S(2)}, u32[]{:S(2)}) async-start(bf16[32,4,4096]{2,1,0:T(4,128)(2,1)} %get-tuple-element.13), calls=%async_computation | async-start | bytes 2097152 | tf_op jit(solution)/shard_map/all_to_all | solution.py:361
  10.7 6.5 %load_weights.1 = (bf16[2,4096,768]{2,1,0:T(8,128)(2,1)S(1)}, bf16[768,4096]{1,0:T(8,128)(2,1)S(1)}) custom-call(bf16[2,4096,768]{2,1,0:T(8,128)(2,1)} %bitcast.4, bf16[768,4096]{1,0:T(8,128)(2,1)} %bitcast.5, bf16[32,128]{1,0:T(8,128)(2,1)S(1)} %get-tuple-element.14.after.place_ref), custom_call_target="tpu_custom_call" | custom-call | bytes 18874368 | tf_op jit(solution)/shard_map/load_weights/pallas_call | solution.py:151
  17.3 0.0 copy-start
  17.3 4.8 %copy-done = bf16[2,4096,768]{2,1,0:T(8,128)(2,1)} copy-done((bf16[2,4096,768]{2,1,0:T(8,128)(2,1)}, bf16[2,4096,768]{2,1,0:T(8,128)(2,1)S(1)}, u32[]{:S(2)}) %copy-start) | copy-done | bytes 12582936
  22.0 0.0 copy-start.2
  22.0 2.7 %copy-done.2 = bf16[768,4096]{1,0:T(8,128)(2,1)} copy-done((bf16[768,4096]{1,0:T(8,128)(2,1)}, bf16[768,4096]{1,0:T(8,128)(2,1)S(1)}, u32[]{:S(2)}) %copy-start.2) | copy-done | bytes 6291480
  24.7 13.2 %all-to-all-done.got = bf16[32,4,4096]{2,1,0:T(4,128)(2,1)S(1)} async-done(((bf16[32,4,4096]{2,1,0:T(4,128)(2,1)}), bf16[32,4,4096]{2,1,0:T(4,128)(2,1)S(1)}, u32[]{:S(2)}, u32[]{:S(2)}) %all-to-all-start) | async-done | bytes 1048608 | tf_op jit(solution)/shard_map/all_to_all | solution.py:361
  37.9 0.0 copy-start.1
  37.9 4.6 %copy-done.1 = bf16[2,4096,768]{2,1,0:T(8,128)(2,1)S(1)} copy-done((bf16[2,4096,768]{2,1,0:T(8,128)(2,1)S(1)}, bf16[2,4096,768]{2,1,0:T(8,128)(2,1)}, u32[]{:S(2)}) %copy-start.1) | copy-done | bytes 12582936
  42.5 0.0 copy-start.3
  42.5 2.8 %copy-done.3 = bf16[768,4096]{1,0:T(8,128)(2,1)S(1)} copy-done((bf16[768,4096]{1,0:T(8,128)(2,1)S(1)}, bf16[768,4096]{1,0:T(8,128)(2,1)}, u32[]{:S(2)}) %copy-start.3) | copy-done | bytes 6291480
  45.3 9.7 %expert_rows.1 = (bf16[64,768]{1,0:T(8,128)(2,1)S(1)}, bf16[64,768]{1,0:T(8,128)(2,1)S(1)}, bf16[64,768]{1,0:T(8,128)(2,1)S(1)}, bf16[64,4096]{1,0:T(8,128)(2,1)...) custom-call(bf16[32,4,4096]{2,1,0:T(4,128)(2,1)S(1)} %all-to-all-done.got, ...), custom_call_target="tpu_custom_call" | custom-call | flops 2013265920 | bytes 18874368 | tf_op jit(solution)/shard_map/expert_rows/pallas_call | solution.py:215
  55.0 2.6 %all-to-all-start.1 = ((bf16[32,2,4096]{2,1,0:T(2,128)(2,1)}), bf16[32,2,4096]{2,1,0:T(2,128)(2,1)S(1)}, u32[]{:S(2)}, u32[]{:S(2)}) async-start(bf16[32,2,4096]{2,1,0:T(2,128)(2,1)} %get-tuple-element.17), calls=%async_computation.1 | async-start | bytes 1048576 | tf_op jit(solution)/shard_map/all_to_all | solution.py:361
  57.7 3.3 %down_grad.1 = bf16[1,768,4096]{2,1,0:T(8,128)(2,1)} custom-call(bf16[64,4096]{1,0:T(8,128)(2,1)S(1)} %get-tuple-element.21.refs_0_, bf16[64,768]{1,0:T(8,128)(2,1)S(1)} %get-tuple-element.22.refs_1_), custom_call_target="tpu_custom_call" | custom-call | flops 402653184 | bytes 6291456 | tf_op jit(solution)/shard_map/down_grad/pallas_call | solution.py:301
  61.0 5.3 %pair_grad.1 = bf16[1,2,4096,768]{3,2,1,0:T(8,128)(2,1)} custom-call(bf16[64,4096]{1,0:T(8,128)(2,1)S(1)} %get-tuple-element.18.refs_0_, bf16[64,768]{1,0:T(8,128)(2,1)S(1)} %get-tuple-element.19.refs_1_, bf16[64,768]{1,0:T(8,128)(2,1)S(1)} %get-tuple-element.20.refs_2_), custom_call_target="tpu_custom_call" | custom-call | flops 805306368 | bytes 12582912 | tf_op jit(solution)/shard_map/pair_grad/pallas_call | solution.py:264
  66.3 7.3 %all-to-all-done.1.rows_ref = bf16[32,2,4096]{2,1,0:T(2,128)(2,1)S(1)} async-done(((bf16[32,2,4096]{2,1,0:T(2,128)(2,1)}), bf16[32,2,4096]{2,1,0:T(2,128)(2,1)S(1)}, u32[]{:S(2)}, u32[]{:S(2)}) %all-to-all-start.1) | async-done | bytes 524320 | tf_op jit(solution)/shard_map/all_to_all | solution.py:361
  73.6 1.4 %spread_rows.1 = bf16[128,4096]{1,0:T(8,128)(2,1)} custom-call(bf16[32,2,4096]{2,1,0:T(2,128)(2,1)S(1)} %all-to-all-done.1.rows_ref, bf16[32,128]{1,0:T(8,128)(2,1)S(1)} %get-tuple-element.14.after.place_ref), custom_call_target="tpu_custom_call" | custom-call | flops 33554432 | bytes 1048576 | tf_op jit(solution)/shard_map/spread_rows/pallas_call | solution.py:340
Async XLA Ops:
  3.4 34.5 %all-to-all-start = ((bf16[32,4,4096]{2,1,0:T(4,128)(2,1)}), bf16[32,4,4096]{2,1,0:T(4,128)(2,1)S(1)}, u32[]{:S(2)}, u32[]{:S(2)}) async-start(bf16[32,4,4096]{2,1,0:T(4,128)(2,1)} %get-tuple-element.13), calls=%async_computation | async-start | bytes 2097152 | tf_op jit(solution)/shard_map/all_to_all | solution.py:361
  17.3 4.8 %copy-start = (bf16[2,4096,768]{2,1,0:T(8,128)(2,1)}, bf16[2,4096,768]{2,1,0:T(8,128)(2,1)S(1)}, u32[]{:S(2)}) copy-start(bf16[2,4096,768]{2,1,0:T(8,128)(2,1)S(1)} %get-tuple-element.15.pair) | copy-start | bytes 37748740
  22.0 2.7 %copy-start.2 = (bf16[768,4096]{1,0:T(8,128)(2,1)}, bf16[768,4096]{1,0:T(8,128)(2,1)S(1)}, u32[]{:S(2)}) copy-start(bf16[768,4096]{1,0:T(8,128)(2,1)S(1)} %get-tuple-element.16.down) | copy-start | bytes 18874372
  37.9 4.6 %copy-start.1 = (bf16[2,4096,768]{2,1,0:T(8,128)(2,1)S(1)}, bf16[2,4096,768]{2,1,0:T(8,128)(2,1)}, u32[]{:S(2)}) copy-start(bf16[2,4096,768]{2,1,0:T(8,128)(2,1)} %copy-done) | copy-start | bytes 37748740
  42.5 2.8 %copy-start.3 = (bf16[768,4096]{1,0:T(8,128)(2,1)S(1)}, bf16[768,4096]{1,0:T(8,128)(2,1)}, u32[]{:S(2)}) copy-start(bf16[768,4096]{1,0:T(8,128)(2,1)} %copy-done.2) | copy-start | bytes 18874372
  55.0 18.5 %all-to-all-start.1 = ((bf16[32,2,4096]{2,1,0:T(2,128)(2,1)}), bf16[32,2,4096]{2,1,0:T(2,128)(2,1)S(1)}, u32[]{:S(2)}, u32[]{:S(2)}) async-start(bf16[32,2,4096]{2,1,0:T(2,128)(2,1)} %get-tuple-element.17), calls=%async_computation.1 | async-start | bytes 1048576 | tf_op jit(solution)/shard_map/all_to_all | solution.py:361
